TPU v7x, 32 devices: a whole 2x2x4 slice. The times are simulated.
32 devices in a mesh: dp: 4 (over y, x), fsdp: 8 (over z, core).
Axes of the slice: x: 2, y: 2, z: 4, core: 2. Of those that a mesh axis runs over, the one named last changes fastest.
Arguments:
- mel: bfloat16 [32768, 80], P(('dp', 'fsdp')), may hold values from -6 to 6
- cotangent: bfloat16 [4096, 512], P(('dp', 'fsdp')), may hold values from -6 to 6
- lengths: int32 [128], replicated, may hold values from 8 to 104, as said below
- assignment: int32 [128], replicated, may hold values from 0 to 31, as said below
- time_spans: int32 [32, 2, 2], P(('dp', 'fsdp')), may hold values from 0 to 984, as said below
- freq_spans: int32 [32, 2, 2], P(('dp', 'fsdp')), may hold values from 0 to 53, as said below
- contexts: int32 [8], replicated, may hold values from 16 to 128
- stem_kernels: bfloat16 [3, 9, 256], P(None, None, ('dp', 'fsdp')), may hold values from -2 to 2
- stem_point: bfloat16 [2, 256, 256], P(None, ('dp', 'fsdp')), may hold values from -0.375 to 0.375
- stem_out: bfloat16 [2560, 512], P(('dp', 'fsdp')), may hold values from -0.125 to 0.125
- ffn_in: bfloat16 [2, 512, 2048], P(None, ('dp', 'fsdp')), may hold values from -0.25 to 0.25
- ffn_out: bfloat16 [2, 2048, 512], P(None, ('dp', 'fsdp')), may hold values from -1 to 1
- qkv: bfloat16 [512, 1536], P(('dp', 'fsdp')), may hold values from -0.25 to 0.25
- attn_out: bfloat16 [512, 512], P(('dp', 'fsdp')), may hold values from -2 to 2
- conv_in: bfloat16 [512, 1024], P(('dp', 'fsdp')), may hold values from -0.25 to 0.25
- conv_depth: bfloat16 [9, 512], P(None, ('dp', 'fsdp')), may hold values from -2 to 2
- conv_out: bfloat16 [512, 512], P(('dp', 'fsdp')), may hold values from -0.75 to 0.75
- norm_gains: bfloat16 [6, 512], P(None, ('dp', 'fsdp')), may hold values from 0.25 to 1.75
- norm_shifts: bfloat16 [5, 512], P(None, ('dp', 'fsdp')), may hold values from -1.5 to 1.5
- final_shift: bfloat16 [512], P(('dp', 'fsdp')), may hold values from -1.5 to 1.5
Outputs:
- activations: bfloat16 [4096, 512], P(('dp', 'fsdp'))
- mel_grad: float32 [32768, 80], P(('dp', 'fsdp'))
- grad_stem_kernels: float32 [3, 9, 256], P(None, None, ('dp', 'fsdp'))
- grad_stem_point: float32 [2, 256, 256], P(None, ('dp', 'fsdp'))
- grad_stem_out: float32 [2560, 512], P(('dp', 'fsdp'))
- grad_ffn_in: float32 [2, 512, 2048], P(None, ('dp', 'fsdp'))
- grad_ffn_out: float32 [2, 2048, 512], P(None, ('dp', 'fsdp'))
- grad_qkv: float32 [512, 1536], P(('dp', 'fsdp'))
- grad_attn_out: float32 [512, 512], P(('dp', 'fsdp'))
- grad_conv_in: float32 [512, 1024], P(('dp', 'fsdp'))
- grad_conv_depth: float32 [9, 512], P(None, ('dp', 'fsdp'))
- grad_conv_out: float32 [512, 512], P(('dp', 'fsdp'))
- grad_norm_gains: float32 [6, 512], P(None, ('dp', 'fsdp'))
- grad_norm_shifts: float32 [5, 512], P(None, ('dp', 'fsdp'))
- grad_final_shift: float32 [512], P(('dp', 'fsdp'))
Inputs may be any that keep to these rules, and one draw needn't show every extreme that they name: Each device holds exactly 4 utterances whose lengths sum to between 64 and 128; some device holds one utterance of the largest length. `assignment`: device numbers d = dp index * 8 + fsdp index; every device receives exactly 4 utterances. `time_spans`: pairs (first input frame counted from the device's first input frame, width); widths are 0 to 40. `freq_spans`: pairs (first bin, width); widths are 0 to 27.
All inputs are finite; a program needn't handle non-finite values.
Results may differ from a plain program's by a relative error of at most 0.033.
Values may be sent and summed in bfloat16 or wider, within the bound.
A program may use at most 320 MiB of HBM per device.

v0:
```python
import jax
import jax.numpy as jnp
from jax import lax
from jax.sharding import PartitionSpec as P

CTX = 128


EPSILON = 1e-05
MASKED_LOGIT = -1e30


def frame_segments(lengths, assignment, device, frames):
    belongs = assignment == device
    own_sizes = jnp.where(belongs, lengths, 0)
    finishes = jnp.cumsum(own_sizes, dtype=jnp.int32)
    beginnings = finishes - own_sizes
    position = jnp.arange(frames, dtype=jnp.int32)[:, None]
    inside = belongs[None, :] & (position >= beginnings[None, :]) & (position < finishes[None, :])
    number = jnp.arange(lengths.shape[0], dtype=jnp.int32)[None, :] + 1
    return jnp.sum(jnp.where(inside, number, 0), axis=1, dtype=jnp.int32) - 1


def feature_keep(segments, time_spans, freq_spans, mel_bins):
    frames = segments.shape[0] * 8
    position = jnp.arange(frames, dtype=jnp.int32)[:, None]
    covered = (position >= time_spans[None, :, 0]) & (
        position < time_spans[None, :, 0] + time_spans[None, :, 1]
    )
    time_keep = jnp.repeat(segments >= 0, 8) & jnp.logical_not(jnp.any(covered, axis=1))
    channel = jnp.arange(mel_bins, dtype=jnp.int32)[:, None]
    banned = (channel >= freq_spans[None, :, 0]) & (
        channel < freq_spans[None, :, 0] + freq_spans[None, :, 1]
    )
    freq_keep = jnp.logical_not(jnp.any(banned, axis=1))
    return (time_keep[:, None] & freq_keep[None, :]).astype(jnp.float32)


def time_taps(values, seg_in, seg_out):
    out_len = seg_out.shape[0]
    paired = values.reshape((out_len, 2) + values.shape[1:])
    even_part = paired[:, 0]
    odd_part = paired[:, 1]
    prior_part = jnp.concatenate([jnp.zeros_like(odd_part[:1]), odd_part[:-1]], axis=0)
    seg_pairs = seg_in.reshape(out_len, 2)
    prior_segs = jnp.concatenate([jnp.full((1,), -2, jnp.int32), seg_pairs[:-1, 1]])
    opening = ((prior_segs == seg_out) & (seg_out >= 0)).astype(values.dtype)
    opening = opening.reshape((out_len,) + (1,) * (values.ndim - 1))
    return (prior_part * opening, even_part, odd_part)


def freq_taps(values):
    frames, bins_in = (values.shape[0], values.shape[1])
    paired = values.reshape((frames, bins_in // 2, 2) + values.shape[2:])
    even_part = paired[:, :, 0]
    odd_part = paired[:, :, 1]
    prior_part = jnp.concatenate([jnp.zeros_like(odd_part[:, :1]), odd_part[:, :-1]], axis=1)
    return (prior_part, even_part, odd_part)


def strided_conv(values, kernel, seg_in, seg_out):
    summed = None
    for tap_row, tap_rows in enumerate(time_taps(values, seg_in, seg_out)):
        for tap_col, tap_piece in enumerate(freq_taps(tap_rows)):
            if tap_piece.ndim == 2:
                tap_piece = tap_piece[:, :, None]
            addend = tap_piece * kernel[3 * tap_row + tap_col]
            summed = addend if summed is None else summed + addend
    present = (seg_out >= 0).astype(summed.dtype)
    return summed * present[:, None, None]


def layer_norm(values, norm_gain, norm_shift):
    average = jnp.mean(values, axis=-1, keepdims=True)
    centred = values - average
    spread = jnp.mean(centred * centred, axis=-1, keepdims=True)
    return centred * lax.rsqrt(spread + EPSILON) * norm_gain + norm_shift


def depth_glu(gated_rows, kernel, segments):
    model_width = gated_rows.shape[1] // 2
    merged = gated_rows[:, :model_width] * jax.nn.sigmoid(gated_rows[:, model_width:])
    radius = kernel.shape[0] // 2
    frames = gated_rows.shape[0]
    padded = jnp.pad(merged, ((radius, radius), (0, 0)))
    padded_segs = jnp.pad(segments, (radius, radius), constant_values=-2)
    summed = jnp.zeros_like(merged)
    for tap_index in range(kernel.shape[0]):
        same_segment = (padded_segs[tap_index : tap_index + frames] == segments).astype(
            merged.dtype
        )
        summed = (
            summed
            + padded[tap_index : tap_index + frames] * same_segment[:, None] * kernel[tap_index]
        )
    return summed


def stem_front(masked, first_kernel, second_kernel, segments):
    seg_zero = jnp.repeat(segments, 8)
    seg_one = jnp.repeat(segments, 4)
    seg_two = jnp.repeat(segments, 2)
    level_one = jax.nn.silu(strided_conv(masked, first_kernel, seg_zero, seg_one))
    return strided_conv(level_one, second_kernel, seg_one, seg_two)


def stem_middle(point_two, third_kernel, segments):
    frames = segments.shape[0]
    channels = point_two.shape[1]
    hidden = jax.nn.silu(point_two).reshape(frames * 2, -1, channels)
    return strided_conv(hidden, third_kernel, jnp.repeat(segments, 2), segments)


def matmul(operand, matrix):
    return jnp.dot(operand, matrix, preferred_element_type=jnp.float32)


def over_rows(operand, matrix):
    return lax.dot_general(
        operand, matrix, (((0,), (0,)), ((), ())), preferred_element_type=jnp.float32
    )


def against(operand, matrix):
    return lax.dot_general(
        operand, matrix, (((1,), (1,)), ((), ())), preferred_element_type=jnp.float32
    )


def ffn_forward(stream, norm_gain, norm_shift, inner_weight, outer_weight):
    normed = layer_norm(stream, norm_gain, norm_shift).astype(jnp.bfloat16)
    hidden = matmul(normed, inner_weight)
    active = jax.nn.silu(hidden).astype(jnp.bfloat16)
    return (matmul(active, outer_weight), (normed, hidden, active))


def ffn_backward(stream, norm_gain, norm_shift, inner_weight, outer_weight, kept_values, grad_out):
    normed, hidden, active = kept_values
    grad_outer = over_rows(active, grad_out)
    grad_active = against(grad_out, outer_weight)
    grad_hidden = jax.vjp(jax.nn.silu, hidden)[1](grad_active)[0].astype(jnp.bfloat16)
    grad_inner = over_rows(normed, grad_hidden)
    grad_normed = against(grad_hidden, inner_weight)
    pullback = jax.vjp(layer_norm, stream, norm_gain, norm_shift)[1]
    grad_stream, grad_gain, grad_shift = pullback(grad_normed)
    return (grad_stream, grad_gain, grad_shift, grad_inner, grad_outer)


def split_heads(joined, head_count):
    frames = joined.shape[0]
    model_width = joined.shape[1] // 3
    shaped = joined.reshape(frames, 3, head_count, model_width // head_count)
    return (shaped[:, 0], shaped[:, 1], shaped[:, 2])


def block_logits(queries, key_rows, query_segs, key_segs, anchor, frames, contexts):
    scores = jnp.einsum("qhd,khd->hqk", queries, key_rows, preferred_element_type=jnp.float32)
    radius = (key_rows.shape[0] - queries.shape[0]) // 2
    query_pos = anchor + jnp.arange(queries.shape[0], dtype=jnp.int32)
    key_pos = anchor - radius + jnp.arange(key_rows.shape[0], dtype=jnp.int32)
    distance = jnp.abs(query_pos[:, None] - key_pos[None, :])
    allowed = (
        (query_segs[:, None] == key_segs[None, :])
        & (key_pos[None, :] >= 0)
        & (key_pos[None, :] < frames)
    )
    allowed = allowed[None] & (distance[None] <= contexts[:, None, None])
    return jnp.where(allowed, scores * queries.shape[2] ** (-0.5), MASKED_LOGIT)


def attend_forward(joined, segments, contexts):
    frames = joined.shape[0]
    queries, key_rows, value_rows = split_heads(joined, contexts.shape[0])
    padded_keys = jnp.pad(key_rows, ((CTX, CTX), (0, 0), (0, 0)))
    padded_values = jnp.pad(value_rows, ((CTX, CTX), (0, 0), (0, 0)))
    padded_segs = jnp.pad(segments, (CTX, CTX), constant_values=-2)
    logits = block_logits(queries, padded_keys, segments, padded_segs, 0, frames, contexts)
    highest = jnp.max(logits, axis=-1, keepdims=True)
    exponent = jnp.exp(logits - highest)
    summed = jnp.sum(exponent, axis=-1, keepdims=True)
    weights = (exponent / summed).astype(jnp.bfloat16)
    outputs = jnp.einsum("hqk,khd->qhd", weights, padded_values, preferred_element_type=jnp.float32)
    log_parts = highest[:, :, 0] + jnp.log(summed[:, :, 0])
    return (outputs, log_parts)


def attend_backward(joined, segments, contexts, log_totals, grad_mixed):
    frames = joined.shape[0]
    queries, key_rows, value_rows = split_heads(joined, contexts.shape[0])
    padded_keys = jnp.pad(key_rows, ((CTX, CTX), (0, 0), (0, 0)))
    padded_values = jnp.pad(value_rows, ((CTX, CTX), (0, 0), (0, 0)))
    padded_segs = jnp.pad(segments, (CTX, CTX), constant_values=-2)
    block_rows = min(frames, 512)
    grad_keys = jnp.zeros(padded_keys.shape, jnp.float32)
    grad_values = jnp.zeros(padded_values.shape, jnp.float32)
    query_span = slice(0, block_rows)
    key_span = slice(0, block_rows + 2 * CTX)
    logits = block_logits(queries, padded_keys, segments, padded_segs, 0, frames, contexts)
    weights = jnp.exp(logits - log_totals[:, query_span, None])
    grad_weights = jnp.einsum(
        "qhd,khd->hqk", grad_mixed, padded_values, preferred_element_type=jnp.float32
    )
    row_dot = jnp.sum(weights * grad_weights, axis=-1, keepdims=True)
    grad_scores = (weights * (grad_weights - row_dot) * queries.shape[2] ** (-0.5)).astype(
        jnp.bfloat16
    )
    grad_queries = jnp.einsum(
        "hqk,khd->qhd", grad_scores, padded_keys, preferred_element_type=jnp.float32
    )
    grad_keys = grad_keys.at[key_span].add(
        jnp.einsum("hqk,qhd->khd", grad_scores, queries, preferred_element_type=jnp.float32)
    )
    grad_values = grad_values.at[key_span].add(
        jnp.einsum(
            "hqk,qhd->khd",
            weights.astype(jnp.bfloat16),
            grad_mixed,
            preferred_element_type=jnp.float32,
        )
    )
    stacked = jnp.stack(
        [grad_queries, grad_keys[CTX : CTX + frames], grad_values[CTX : CTX + frames]], axis=1
    )
    return stacked.reshape(frames, -1)


def local(
    mel,
    cotangent,
    lengths,
    assignment,
    time_spans,
    freq_spans,
    contexts,
    stem_kernels,
    stem_point,
    stem_out,
    ffn_in,
    ffn_out,
    qkv,
    attn_out,
    conv_in,
    conv_depth,
    conv_out,
    norm_gains,
    norm_shifts,
    final_shift,
):
    device = lax.axis_index("dp") * lax.axis_size("fsdp") + lax.axis_index("fsdp")
    frames = cotangent.shape[0]
    segments = frame_segments(lengths, assignment, device, frames)
    feature_mask = feature_keep(segments, time_spans[0], freq_spans[0], mel.shape[1])
    present = (segments >= 0).astype(jnp.float32)[:, None]
    counted = jnp.sum(lengths).astype(jnp.float32)
    gathered = (
        lax.all_gather(stem_kernels, ("dp", "fsdp"), axis=2, tiled=True),
        lax.all_gather(stem_point, ("dp", "fsdp"), axis=1, tiled=True),
        lax.all_gather(stem_out, ("dp", "fsdp"), axis=0, tiled=True),
        lax.all_gather(ffn_in, ("dp", "fsdp"), axis=1, tiled=True),
        lax.all_gather(ffn_out, ("dp", "fsdp"), axis=1, tiled=True),
        lax.all_gather(qkv, ("dp", "fsdp"), axis=0, tiled=True),
        lax.all_gather(attn_out, ("dp", "fsdp"), axis=0, tiled=True),
        lax.all_gather(conv_in, ("dp", "fsdp"), axis=0, tiled=True),
        lax.all_gather(conv_depth, ("dp", "fsdp"), axis=1, tiled=True),
        lax.all_gather(conv_out, ("dp", "fsdp"), axis=0, tiled=True),
        lax.all_gather(norm_gains, ("dp", "fsdp"), axis=1, tiled=True),
        lax.all_gather(norm_shifts, ("dp", "fsdp"), axis=1, tiled=True),
        lax.all_gather(final_shift, ("dp", "fsdp"), axis=0, tiled=True),
    )
    (
        kernels,
        point_weight,
        stem_weight,
        ffn_inner,
        ffn_outer,
        qkv_weight,
        out_weight,
        conv_inner,
        conv_taps,
        conv_outer,
        norm_rows,
        shift_rows,
        final_row,
    ) = gathered
    kernels_wide = kernels.astype(jnp.float32)
    gains_wide = norm_rows.astype(jnp.float32)
    shifts_wide = shift_rows.astype(jnp.float32)
    final_wide = final_row.astype(jnp.float32)
    masked = mel.astype(jnp.float32) * feature_mask
    level_two, front_pullback = jax.vjp(
        lambda masked_input, first_taps, second_taps: stem_front(
            masked_input, first_taps, second_taps, segments
        ),
        masked,
        kernels_wide[0],
        kernels_wide[1],
    )
    channels = level_two.shape[2]
    level_two_low = level_two.reshape(-1, channels).astype(jnp.bfloat16)
    point_two = matmul(level_two_low, point_weight[0])
    level_three, middle_pullback = jax.vjp(
        lambda point_input, third_taps: stem_middle(point_input, third_taps, segments),
        point_two,
        kernels_wide[2],
    )
    level_three_low = level_three.reshape(-1, channels).astype(jnp.bfloat16)
    point_three = matmul(level_three_low, point_weight[1])
    stem_hidden = jax.nn.silu(point_three).reshape(frames, -1).astype(jnp.bfloat16)
    after_stem = matmul(stem_hidden, stem_weight)
    ffn_result_one, ffn_kept_one = ffn_forward(
        after_stem, gains_wide[0], shifts_wide[0], ffn_inner[0], ffn_outer[0]
    )
    after_ffn = after_stem + 0.5 * ffn_result_one
    attn_normed = layer_norm(after_ffn, gains_wide[1], shifts_wide[1]).astype(jnp.bfloat16)
    joined = matmul(attn_normed, qkv_weight).astype(jnp.bfloat16)
    mixed_heads, log_totals = attend_forward(joined, segments, contexts)
    mixed_low = mixed_heads.reshape(frames, -1).astype(jnp.bfloat16)
    after_attn = after_ffn + matmul(mixed_low, out_weight)
    conv_normed = layer_norm(after_attn, gains_wide[2], shifts_wide[2]).astype(jnp.bfloat16)
    gated_rows = matmul(conv_normed, conv_inner)
    taps_wide = conv_taps.astype(jnp.float32)
    depthwise, depth_pullback = jax.vjp(
        lambda gate_input, taps_input: depth_glu(gate_input, taps_input, segments),
        gated_rows,
        taps_wide,
    )
    first_sum, second_sum = lax.psum(
        (jnp.sum(depthwise * present, axis=0), jnp.sum(depthwise * depthwise * present, axis=0)),
        ("dp", "fsdp"),
    )
    average = first_sum / counted
    spread = second_sum / counted - average * average
    inv_spread = lax.rsqrt(spread + EPSILON)
    standard = (depthwise - average) * inv_spread
    batch_normed = standard * gains_wide[3] + shifts_wide[3]
    conv_active = jax.nn.silu(batch_normed).astype(jnp.bfloat16)
    after_conv = after_attn + matmul(conv_active, conv_outer)
    ffn_result_two, ffn_kept_two = ffn_forward(
        after_conv, gains_wide[4], shifts_wide[4], ffn_inner[1], ffn_outer[1]
    )
    after_second = after_conv + 0.5 * ffn_result_two
    activations = (layer_norm(after_second, gains_wide[5], final_wide) * present).astype(
        jnp.bfloat16
    )
    weights_back = (
        lax.all_gather(stem_kernels, ("dp", "fsdp"), axis=2, tiled=True),
        lax.all_gather(stem_point, ("dp", "fsdp"), axis=1, tiled=True),
        lax.all_gather(stem_out, ("dp", "fsdp"), axis=0, tiled=True),
        lax.all_gather(ffn_in, ("dp", "fsdp"), axis=1, tiled=True),
        lax.all_gather(ffn_out, ("dp", "fsdp"), axis=1, tiled=True),
        lax.all_gather(qkv, ("dp", "fsdp"), axis=0, tiled=True),
        lax.all_gather(attn_out, ("dp", "fsdp"), axis=0, tiled=True),
        lax.all_gather(conv_in, ("dp", "fsdp"), axis=0, tiled=True),
        lax.all_gather(conv_depth, ("dp", "fsdp"), axis=1, tiled=True),
        lax.all_gather(conv_out, ("dp", "fsdp"), axis=0, tiled=True),
        lax.all_gather(norm_gains, ("dp", "fsdp"), axis=1, tiled=True),
        lax.all_gather(norm_shifts, ("dp", "fsdp"), axis=1, tiled=True),
        lax.all_gather(final_shift, ("dp", "fsdp"), axis=0, tiled=True),
    )
    (
        back_kernels,
        back_point,
        back_stem,
        back_inner,
        back_outer,
        back_qkv,
        back_attn,
        back_conv_in,
        back_taps,
        back_conv_out,
        back_gains,
        back_shifts,
        back_final,
    ) = weights_back
    back_gains_wide = back_gains.astype(jnp.float32)
    back_shifts_wide = back_shifts.astype(jnp.float32)
    back_final_wide = back_final.astype(jnp.float32)
    grad_final = cotangent.astype(jnp.float32) * present
    pullback = jax.vjp(layer_norm, after_second, back_gains_wide[5], back_final_wide)[1]
    grad_stream, grad_gain_final, grad_shift_final = pullback(grad_final)
    ffn_two = ffn_backward(
        after_conv,
        back_gains_wide[4],
        back_shifts_wide[4],
        back_inner[1],
        back_outer[1],
        ffn_kept_two,
        (0.5 * grad_stream).astype(jnp.bfloat16),
    )
    grad_stream = grad_stream + ffn_two[0]
    grad_conv_low = grad_stream.astype(jnp.bfloat16)
    grad_conv_out = over_rows(conv_active, grad_conv_low)
    grad_active = against(grad_conv_low, back_conv_out)
    grad_batch = jax.vjp(jax.nn.silu, batch_normed)[1](grad_active)[0]
    beta_sum, gamma_sum = lax.psum(
        (jnp.sum(grad_batch * present, axis=0), jnp.sum(grad_batch * standard * present, axis=0)),
        ("dp", "fsdp"),
    )
    bn_gain = back_gains_wide[3]
    grad_first = (
        inv_spread * inv_spread * bn_gain * gamma_sum * average - inv_spread * bn_gain * beta_sum
    ) / counted
    grad_second = -0.5 * inv_spread * inv_spread * bn_gain * gamma_sum / counted
    grad_depth = bn_gain * inv_spread * grad_batch + present * (
        grad_first + 2.0 * depthwise * grad_second
    )
    grad_gated, grad_taps = depth_pullback(grad_depth)
    grad_gated_low = grad_gated.astype(jnp.bfloat16)
    grad_conv_in = over_rows(conv_normed, grad_gated_low)
    pullback = jax.vjp(layer_norm, after_attn, back_gains_wide[2], back_shifts_wide[2])[1]
    conv_norm_grads = pullback(against(grad_gated_low, back_conv_in))
    grad_stream = grad_stream + conv_norm_grads[0]
    grad_attn_low = grad_stream.astype(jnp.bfloat16)
    grad_attn_out = over_rows(mixed_low, grad_attn_low)
    grad_mixed = against(grad_attn_low, back_attn).astype(jnp.bfloat16).reshape(mixed_heads.shape)
    grad_joined = attend_backward(joined, segments, contexts, log_totals, grad_mixed).astype(
        jnp.bfloat16
    )
    grad_qkv = over_rows(attn_normed, grad_joined)
    pullback = jax.vjp(layer_norm, after_ffn, back_gains_wide[1], back_shifts_wide[1])[1]
    attn_norm_grads = pullback(against(grad_joined, back_qkv))
    grad_stream = grad_stream + attn_norm_grads[0]
    ffn_one = ffn_backward(
        after_stem,
        back_gains_wide[0],
        back_shifts_wide[0],
        back_inner[0],
        back_outer[0],
        ffn_kept_one,
        (0.5 * grad_stream).astype(jnp.bfloat16),
    )
    grad_stream = grad_stream + ffn_one[0]
    grad_stem_low = grad_stream.astype(jnp.bfloat16)
    grad_stem_out = over_rows(stem_hidden, grad_stem_low)
    grad_hidden = against(grad_stem_low, back_stem).reshape(point_three.shape)
    grad_point_three = jax.vjp(jax.nn.silu, point_three)[1](grad_hidden)[0].astype(jnp.bfloat16)
    grad_third_point = over_rows(level_three_low, grad_point_three)
    grad_level_three = against(grad_point_three, back_point[1]).reshape(level_three.shape)
    grad_point_two, grad_third_kernel = middle_pullback(grad_level_three)
    grad_point_two_low = grad_point_two.astype(jnp.bfloat16)
    grad_second_point = over_rows(level_two_low, grad_point_two_low)
    grad_level_two = against(grad_point_two_low, back_point[0]).reshape(level_two.shape)
    grad_masked, grad_first_kernel, grad_second_kernel = front_pullback(grad_level_two)
    mel_grad = grad_masked * feature_mask
    zero_row = jnp.zeros_like(grad_gain_final)
    grad_gains = jnp.stack(
        [ffn_one[1], attn_norm_grads[1], conv_norm_grads[1], zero_row, ffn_two[1], grad_gain_final]
    )
    grad_shifts = jnp.stack(
        [ffn_one[2], attn_norm_grads[2], conv_norm_grads[2], zero_row, ffn_two[2]]
    )
    grad_kernels = jnp.stack([grad_first_kernel, grad_second_kernel, grad_third_kernel])
    grad_points = jnp.stack([grad_second_point, grad_third_point])
    grad_inner = jnp.stack([ffn_one[3], ffn_two[3]])
    grad_outer = jnp.stack([ffn_one[4], ffn_two[4]])
    owned_grads = (
        lax.psum_scatter(grad_kernels, ("dp", "fsdp"), scatter_dimension=2, tiled=True),
        lax.psum_scatter(grad_points, ("dp", "fsdp"), scatter_dimension=1, tiled=True),
        lax.psum_scatter(grad_stem_out, ("dp", "fsdp"), scatter_dimension=0, tiled=True),
        lax.psum_scatter(grad_inner, ("dp", "fsdp"), scatter_dimension=1, tiled=True),
        lax.psum_scatter(grad_outer, ("dp", "fsdp"), scatter_dimension=1, tiled=True),
        lax.psum_scatter(grad_qkv, ("dp", "fsdp"), scatter_dimension=0, tiled=True),
        lax.psum_scatter(grad_attn_out, ("dp", "fsdp"), scatter_dimension=0, tiled=True),
        lax.psum_scatter(grad_conv_in, ("dp", "fsdp"), scatter_dimension=0, tiled=True),
        lax.psum_scatter(grad_taps, ("dp", "fsdp"), scatter_dimension=1, tiled=True),
        lax.psum_scatter(grad_conv_out, ("dp", "fsdp"), scatter_dimension=0, tiled=True),
        lax.psum_scatter(grad_gains, ("dp", "fsdp"), scatter_dimension=1, tiled=True),
        lax.psum_scatter(grad_shifts, ("dp", "fsdp"), scatter_dimension=1, tiled=True),
        lax.psum_scatter(grad_shift_final, ("dp", "fsdp"), scatter_dimension=0, tiled=True),
    )
    share_width = gamma_sum.shape[0] // (lax.axis_size("dp") * lax.axis_size("fsdp"))
    own_gamma = lax.dynamic_slice_in_dim(gamma_sum, device * share_width, share_width)
    own_beta = lax.dynamic_slice_in_dim(beta_sum, device * share_width, share_width)
    owned_gains = owned_grads[10].at[3].add(own_gamma)
    owned_shifts = owned_grads[11].at[3].add(own_beta)
    return (
        activations,
        mel_grad,
        owned_grads[0],
        owned_grads[1],
        owned_grads[2],
        owned_grads[3],
        owned_grads[4],
        owned_grads[5],
        owned_grads[6],
        owned_grads[7],
        owned_grads[8],
        owned_grads[9],
        owned_gains,
        owned_shifts,
        owned_grads[12],
    )


def solution(mesh):
    return jax.shard_map(
        local,
        mesh=mesh,
        in_specs=(
            P(("dp", "fsdp"), None),
            P(("dp", "fsdp"), None),
            P(),
            P(),
            P(("dp", "fsdp"), None, None),
            P(("dp", "fsdp"), None, None),
            P(),
            P(None, None, ("dp", "fsdp")),
            P(None, ("dp", "fsdp"), None),
            P(("dp", "fsdp"), None),
            P(None, ("dp", "fsdp"), None),
            P(None, ("dp", "fsdp"), None),
            P(("dp", "fsdp"), None),
            P(("dp", "fsdp"), None),
            P(("dp", "fsdp"), None),
            P(None, ("dp", "fsdp")),
            P(("dp", "fsdp"), None),
            P(None, ("dp", "fsdp")),
            P(None, ("dp", "fsdp")),
            P(("dp", "fsdp")),
        ),
        out_specs=(
            P(("dp", "fsdp"), None),
            P(("dp", "fsdp"), None),
            P(None, None, ("dp", "fsdp")),
            P(None, ("dp", "fsdp"), None),
            P(("dp", "fsdp"), None),
            P(None, ("dp", "fsdp"), None),
            P(None, ("dp", "fsdp"), None),
            P(("dp", "fsdp"), None),
            P(("dp", "fsdp"), None),
            P(("dp", "fsdp"), None),
            P(None, ("dp", "fsdp")),
            P(("dp", "fsdp"), None),
            P(None, ("dp", "fsdp")),
            P(None, ("dp", "fsdp")),
            P(("dp", "fsdp")),
        ),
        check_vma=False,
    )
```

profile of v0, /device:TPU:0, one launch (start us, length us, event | category | flops | bytes accessed | tf_op | source)
XLA Modules:
  0.0 2156.5 jit_solution(17925771221268386645)
XLA Ops:
  11.8 44.3 %all_gather.48 = bf16[3,9,256]{1,2,0:T(8,128)(2,1)S(1)} all-gather(bf16[3,9,8]{1,2,0:T(8,128)(2,1)} %param.39), channel_id=1, replica_groups=mesh['dp'=4,'fsdp'=8] {'dp','fsdp'}, dimensions={2}, use_global_device_ids=true | all-gather | bytes 14256 | tf_op jit(solution)/shard_map/all_gather | solution.py:256
  67.5 27.2 %fusion.4 = f32[256,2,40,256]{3,0,2,1:T(8,128)} fusion(f32[256]{0:T(256)S(1)} %get-tuple-element.347, f32[256]{0:T(256)S(1)} %get-tuple-element.235, f32[256,2,40]{0,2,1:T(8,128)S(1)} %copy.354, f32[256]{0:T(256)S(1)} %get-tuple-element.237, f32[256,2,40]{0,2,1:T(8,128)S(1)} %copy.352, f32[256]{0:T(256)S(1)} %get-tuple-element.238, ...), kind=kLoop, calls=%fused_computation.24 | loop fusion | flops 115343360 | bytes 21719040 | tf_op jit(solution)/shard_map/jvp(jit(silu))/mul | solution.py:103
  112.3 38.5 %all_gather.49 = bf16[2,256,256]{2,1,0:T(8,128)(2,1)S(1)} all-gather(bf16[2,8,256]{2,1,0:T(8,128)(2,1)S(1)} %copy-done.199), channel_id=1, replica_groups=mesh['dp'=4,'fsdp'=8] {'dp','fsdp'}, dimensions={1}, use_global_device_ids=true | all-gather | bytes 270336 | tf_op jit(solution)/shard_map/all_gather | solution.py:257
  169.1 19.4 multiply_convert_fusion
  216.3 39.8 %all-reduce.100 = bf16[512]{0:T(512)(128)(2,1)S(1)} all-reduce(bf16[512]{0:T(512)(128)(2,1)S(1)} %dynamic-update-slice.10), channel_id=1, replica_groups=mesh['dp'=4,'fsdp'=8] {'dp','fsdp'}, use_global_device_ids=true, to_apply=%add.100 | all-reduce | flops 512 | bytes 2048
  258.7 40.2 %all-gather = bf16[32,16,6]{1,2,0:T(8,128)(2,1)S(1)} all-gather(bf16[1,16,6]{1,2,0:T(8,128)(2,1)S(1)} %bitcast.553), channel_id=1, replica_groups=mesh['dp'=4,'fsdp'=8] {'dp','fsdp'}, dimensions={0}, use_global_device_ids=true | all-gather | bytes 6336 | tf_op jit(solution)/shard_map/all_gather | solution.py:266
  299.0 36.9 %all-gather.1 = bf16[32,16,5]{1,2,0:T(8,128)(2,1)S(1)} all-gather(bf16[1,16,5]{1,2,0:T(8,128)(2,1)S(1)} %bitcast.554), channel_id=1, replica_groups=mesh['dp'=4,'fsdp'=8] {'dp','fsdp'}, dimensions={0}, use_global_device_ids=true | all-gather | bytes 5280 | tf_op jit(solution)/shard_map/all_gather | solution.py:267
  337.6 38.5 %all_gather.58 = bf16[9,512]{0,1:T(8,128)(2,1)S(1)} all-gather(bf16[9,16]{0,1:T(8,128)(2,1)S(1)} %copy.377), channel_id=1, replica_groups=mesh['dp'=4,'fsdp'=8] {'dp','fsdp'}, dimensions={1}, use_global_device_ids=true | all-gather | bytes 9504 | tf_op jit(solution)/shard_map/all_gather | solution.py:264
  379.4 41.5 %all_gather.56 = bf16[512,512]{1,0:T(8,128)(2,1)} all-gather(bf16[16,512]{1,0:T(8,128)(2,1)S(1)} %copy-done.115), channel_id=1, replica_groups=mesh['dp'=4,'fsdp'=8] {'dp','fsdp'}, dimensions={0}, use_global_device_ids=true | all-gather | bytes 540672 | tf_op jit(solution)/shard_map/all_gather | solution.py:262
  420.8 42.9 %all_gather.59 = bf16[512,512]{1,0:T(8,128)(2,1)} all-gather(bf16[16,512]{1,0:T(8,128)(2,1)} %param.48), channel_id=1, replica_groups=mesh['dp'=4,'fsdp'=8] {'dp','fsdp'}, dimensions={0}, use_global_device_ids=true | all-gather | bytes 540672 | tf_op jit(solution)/shard_map/all_gather | solution.py:265
  511.3 38.2 %all-reduce.105 = (f32[512]{0:T(512)}, f32[512]{0:T(512)}) all-reduce(f32[512]{0:T(512)} %get-tuple-element.247, f32[512]{0:T(512)} %get-tuple-element.246), channel_id=1, replica_groups=mesh['dp'=4,'fsdp'=8] {'dp','fsdp'}, use_global_device_ids=true, to_apply=%region_16.17 | all-reduce | flops 1024 | bytes 8192 | tf_op jit(solution)/shard_map/psum | solution.py:327
  563.0 41.6 %all-reduce.104 = (f32[512]{0:T(512)}, f32[512]{0:T(512)}) all-reduce(f32[512]{0:T(512)} %get-tuple-element.245, f32[512]{0:T(512)S(1)} %get-tuple-element.244), channel_id=1, replica_groups=mesh['dp'=4,'fsdp'=8] {'dp','fsdp'}, use_global_device_ids=true, to_apply=%region_26.27 | all-reduce | flops 1024 | bytes 8192 | tf_op jit(solution)/shard_map/psum | solution.py:395
  741.8 35.1 %multiply_reduce_fusion.26 = (f32[256]{0:T(256)S(1)}, f32[256]{0:T(256)S(1)}, f32[256]{0:T(256)S(1)}, f32[256]{0:T(256)S(1)}, f32[256]{0:T(256)S(1)}, /*index=5*...) fusion(f32[256,20,256]{2,0,1:T(8,128)} %broadcast_multiply_fusi, ...), kind=kLoop, calls=%fused_computation.53 | loop fusion | flops 35387136 | bytes 98057216 | tf_op jit(solution)/shard_map/transpose(jvp())/reduce_sum | solution.py:67
  837.8 64.4 %multiply_reduce_fusion.8 = (f32[256]{0:T(256)S(1)}, f32[256]{0:T(256)S(1)}, f32[256]{0:T(256)S(1)}, f32[256]{0:T(256)S(1)}, f32[256]{0:T(256)S(1)}, /*index=5*/...) fusion(f32[256,2,40]{0,2,1:T(8,128)S(1)} %copy-done.63, ...), kind=kLoop, calls=%fused_computation.13 | loop fusion | flops 340600576 | bytes 22465536 | tf_op jit(solution)/shard_map/transpose(jvp())/reduce_sum | solution.py:67
  907.3 46.4 %all-reduce.103 = (f32[3,9,256]{1,0,2:T(4,128)S(1)}, f32[512]{0:T(512)S(1)}) all-reduce(f32[3,9,256]{1,0,2:T(4,128)S(1)} %copy.401, f32[512]{0:T(512)S(1)} %copy-done.177), channel_id=2, replica_groups=mesh['dp'=4,'fsdp'=8] {'dp','fsdp'}, use_global_device_ids=true, to_apply=%region_72.73.clone | all-reduce | flops 7424 | bytes 59392
  958.0 98.8 %reduce-scatter.34.cloned.1.call-done = f32[16,9]{1,0:T(8,128)} async-done(((f32[512,9]{1,0:T(8,128)}), f32[16,9]{1,0:T(8,128)}) %reduce-scatter.34.cloned.1.call-update) | async-done | bytes 592
  1058.1 131.3 %reduce-scatter.18.cloned.1.call-done = f32[2,8,256]{2,1,0:T(8,128)} async-done(((f32[2,256,256]{2,1,0:T(8,128)}), f32[2,8,256]{2,1,0:T(8,128)}) %reduce-scatter.18.cloned.1.call-update) | async-done | bytes 16400 | tf_op jit(solution)/shard_map/reduce_scatter | solution.py:458
  1189.5 134.0 %reduce-scatter.32.cloned.1.call-done = f32[16,512]{1,0:T(8,128)} async-done(((f32[512,512]{1,0:T(8,128)}), f32[16,512]{1,0:T(8,128)}) %reduce-scatter.32.cloned.1.call-update) | async-done | bytes 32784 | tf_op jit(solution)/shard_map/reduce_scatter | solution.py:466
  1323.5 134.0 %reduce-scatter.28.cloned.1.call-done = f32[16,512]{1,0:T(8,128)} async-done(((f32[512,512]{1,0:T(8,128)}), f32[16,512]{1,0:T(8,128)}) %reduce-scatter.28.cloned.1.call-update) | async-done | bytes 32784 | tf_op jit(solution)/shard_map/reduce_scatter | solution.py:463
  1457.5 136.5 %reduce-scatter.30.cloned.1.call-done = f32[16,1024]{1,0:T(8,128)} async-done(((f32[512,1024]{1,0:T(8,128)}), f32[16,1024]{1,0:T(8,128)}) %reduce-scatter.30.cloned.1.call-update) | async-done | bytes 65552 | tf_op jit(solution)/shard_map/reduce_scatter | solution.py:464
  1594.0 104.5 %reduce-scatter.26.cloned.1.call-done = f32[16,1536]{1,0:T(8,128)} async-done(((f32[512,1536]{1,0:T(8,128)}), f32[16,1536]{1,0:T(8,128)}) %reduce-scatter.26.cloned.1.call-update) | async-done | bytes 98320 | tf_op jit(solution)/shard_map/reduce_scatter | solution.py:462
  1698.5 147.0 %reduce-scatter.20.cloned.1.call-done = f32[80,512]{1,0:T(8,128)} async-done(((f32[2560,512]{1,0:T(8,128)}), f32[80,512]{1,0:T(8,128)}) %reduce-scatter.20.cloned.1.call-update) | async-done | bytes 163856 | tf_op jit(solution)/shard_map/reduce_scatter | solution.py:459
  1845.5 151.3 %reduce-scatter.24.cloned.1.call-done = f32[2,64,512]{2,1,0:T(8,128)} async-done(((f32[2,2048,512]{2,1,0:T(8,128)}), f32[2,64,512]{2,1,0:T(8,128)}) %reduce-scatter.24.cloned.1.call-update) | async-done | bytes 262160 | tf_op jit(solution)/shard_map/reduce_scatter | solution.py:461
  1996.8 152.7 %reduce-scatter.22.cloned.1.call-done = f32[2,16,2048]{2,1,0:T(8,128)} async-done(((f32[2,512,2048]{2,1,0:T(8,128)}), f32[2,16,2048]{2,1,0:T(8,128)}) %reduce-scatter.22.cloned.1.call-update) | async-done | bytes 262160 | tf_op jit(solution)/shard_map/reduce_scatter | solution.py:460
  (816 shorter events, 352.5 us)
Async XLA Ops:
  7.2 474.9 %all-gather.8.cloned.1.call-start = ((), (), s32[]{:S(2)}) async-start(), calls=%async_computation.11 | async-start | bytes 2703360 | tf_op jit(solution)/shard_map/all_gather | solution.py:258
  8.0 478.3 %all-gather.10.cloned.1.call-start = ((), (), s32[]{:S(2)}) async-start(), calls=%async_computation.12 | async-start | bytes 4325376 | tf_op jit(solution)/shard_map/all_gather | solution.py:259
  8.7 480.7 %all-gather.12.cloned.1.call-start = ((), (), s32[]{:S(2)}) async-start(), calls=%async_computation.13 | async-start | bytes 4325376 | tf_op jit(solution)/shard_map/all_gather | solution.py:260
  9.4 484.3 %all-gather.14.cloned.1.call-start = ((), (), s32[]{:S(2)}) async-start(), calls=%async_computation.14 | async-start | bytes 1622016 | tf_op jit(solution)/shard_map/all_gather | solution.py:261
  10.0 495.4 %all-gather.16.cloned.1.call-start = ((), (), s32[]{:S(2)}) async-start(), calls=%async_computation.15 | async-start | bytes 1081344 | tf_op jit(solution)/shard_map/all_gather | solution.py:263
  10.6 944.3 %reduce-scatter.38.cloned.1.call-start = ((), (), s32[]{:S(2)}) async-start(), calls=%async_computation.26 | async-start | bytes 270336
  61.4 409.9 %copy-start.99 = (f32[128]{0:T(128)}, f32[128]{0:T(128)S(1)}, u32[]{:S(2)}) copy-start(f32[128]{0:T(128)S(1)} %get-tuple-element.358) | copy-start | bytes 1540
  150.8 325.8 %copy-start.58 = (bf16[2,256,256]{2,1,0:T(8,128)(2,1)}, bf16[2,256,256]{2,1,0:T(8,128)(2,1)S(1)}, u32[]{:S(2)}) copy-start(bf16[2,256,256]{2,1,0:T(8,128)(2,1)S(1)} %all_gather.49) | copy-start | bytes 786436
  337.6 223.4 %copy-start.93 = (f32[1,512]{1,0:T(1,128)}, f32[1,512]{1,0:T(1,128)S(1)}, u32[]{:S(2)}) copy-start(f32[1,512]{1,0:T(1,128)S(1)} %get-tuple-element.333) | copy-start | bytes 6148
  337.6 274.1 %copy-start.91 = (f32[1,512]{1,0:T(1,128)}, f32[1,512]{1,0:T(1,128)S(1)}, u32[]{:S(2)}) copy-start(f32[1,512]{1,0:T(1,128)S(1)} %get-tuple-element.335) | copy-start | bytes 6148
  337.6 308.2 %copy-start.89 = (f32[1,512]{1,0:T(1,128)}, f32[1,512]{1,0:T(1,128)S(1)}, u32[]{:S(2)}) copy-start(f32[1,512]{1,0:T(1,128)S(1)} %get-tuple-element.336) | copy-start | bytes 6148
  337.6 313.7 %copy-start.95 = (f32[1,512]{1,0:T(1,128)}, f32[1,512]{1,0:T(1,128)S(1)}, u32[]{:S(2)}) copy-start(f32[1,512]{1,0:T(1,128)S(1)} %get-tuple-element.337) | copy-start | bytes 6148
  659.0 297.5 %reduce-scatter.36.cloned.1.call-start = ((), (), s32[]{:S(2)}) async-start(), calls=%async_computation.25 | async-start | bytes 270336
  697.6 359.1 %reduce-scatter.34.cloned.1.call-start = ((), (), s32[]{:S(2)}) async-start(), calls=%async_computation.24 | async-start | bytes 270336
  698.7 490.8 %reduce-scatter.18.cloned.1.call-start = ((), (), s32[]{:S(2)}) async-start(), calls=%async_computation.16 | async-start | bytes 540672 | tf_op jit(solution)/shard_map/reduce_scatter | solution.py:458
  700.6 622.9 %reduce-scatter.32.cloned.1.call-start = ((), (), s32[]{:S(2)}) async-start(), calls=%async_computation.23 | async-start | bytes 1081344 | tf_op jit(solution)/shard_map/reduce_scatter | solution.py:466
  702.1 755.4 %reduce-scatter.28.cloned.1.call-start = ((), (), s32[]{:S(2)}) async-start(), calls=%async_computation.21 | async-start | bytes 1081344 | tf_op jit(solution)/shard_map/reduce_scatter | solution.py:463
  703.5 890.6 %reduce-scatter.30.cloned.1.call-start = ((), (), s32[]{:S(2)}) async-start(), calls=%async_computation.22 | async-start | bytes 2162688 | tf_op jit(solution)/shard_map/reduce_scatter | solution.py:464
  705.4 993.1 %reduce-scatter.26.cloned.1.call-start = ((), (), s32[]{:S(2)}) async-start(), calls=%async_computation.20 | async-start | bytes 3244032 | tf_op jit(solution)/shard_map/reduce_scatter | solution.py:462
  708.1 1137.4 %reduce-scatter.20.cloned.1.call-start = ((), (), s32[]{:S(2)}) async-start(), calls=%async_computation.17 | async-start | bytes 5406720 | tf_op jit(solution)/shard_map/reduce_scatter | solution.py:459
  711.4 1285.4 %reduce-scatter.24.cloned.1.call-start = ((), (), s32[]{:S(2)}) async-start(), calls=%async_computation.19 | async-start | bytes 8650752 | tf_op jit(solution)/shard_map/reduce_scatter | solution.py:461
  718.5 1431.0 %reduce-scatter.22.cloned.1.call-start = ((), (), s32[]{:S(2)}) async-start(), calls=%async_computation.18 | async-start | bytes 8650752 | tf_op jit(solution)/shard_map/reduce_scatter | solution.py:460
  956.4 1193.0 %copy-start.206 = (f32[5,16]{1,0:T(8,128)}, f32[5,16]{1,0:T(8,128)S(1)}, u32[]{:S(2)}) copy-start(f32[5,16]{1,0:T(8,128)S(1)} %scatter-add.9) | copy-start | bytes 964
  958.0 1191.5 %copy-start.205 = (f32[6,16]{1,0:T(8,128)}, f32[6,16]{1,0:T(8,128)S(1)}, u32[]{:S(2)}) copy-start(f32[6,16]{1,0:T(8,128)S(1)} %scatter-add.6) | copy-start | bytes 1156
  (237 other events, 3403.1 us)
Sparse Core Ops, SparseCore 0:
  10.9 60.8 all-gather.7
  74.9 61.2 all-gather.9
  139.3 60.6 all-gather.11
  202.8 53.6 all-gather.13
  259.4 52.6 all-gather.15
  659.1 133.4 reduce-scatter.37
  794.9 129.7 reduce-scatter.35
  926.9 129.7 reduce-scatter.33
  1059.7 129.7 reduce-scatter.17
  1192.1 131.3 reduce-scatter.31
  1326.4 131.0 reduce-scatter.27
  1460.2 133.7 reduce-scatter.29
  1600.9 97.5 reduce-scatter.25
  1701.3 144.0 reduce-scatter.19
  1848.3 148.4 reduce-scatter.23
  1999.6 149.7 reduce-scatter.21
where the time goes:
time: 2170 us; the launch traced here: 2160 us
  waiting for transfers between devices  1190 us (55%)
  blocking collectives  449 us (21%)
  other arithmetic  256 us (12%)
  local copies, waits for them, and re-layouts  148 us (7%)
  matrix products  90.6 us (4%)
    reduce_scatter x1, waiting for transfers between devices, local(): lax.psum_scatter(grad_inner, ('dp', 'fsdp'), scatter_dimension=1, tiled=T...  153 us
    reduce_scatter x1, waiting for transfers between devices, local(): lax.psum_scatter(grad_outer, ('dp', 'fsdp'), scatter_dimension=1, tiled=T...  151 us
    reduce_scatter x1, waiting for transfers between devices, local(): lax.psum_scatter(grad_stem_out, ('dp', 'fsdp'), scatter_dimension=0, tile...  147 us
    reduce_scatter x1, waiting for transfers between devices, local(): lax.psum_scatter(grad_conv_in, ('dp', 'fsdp'), scatter_dimension=0, tiled...  136 us
    reduce_scatter x1, waiting for transfers between devices, local(): lax.psum_scatter(grad_attn_out, ('dp', 'fsdp'), scatter_dimension=0, tile...  134 us
    reduce_scatter x1, waiting for transfers between devices, local(): lax.psum_scatter(grad_conv_out, ('dp', 'fsdp'), scatter_dimension=0, tile...  134 us
    reduce_scatter x1, waiting for transfers between devices, local(): lax.psum_scatter(grad_points, ('dp', 'fsdp'), scatter_dimension=1, tiled=...  131 us
    reduce_scatter x1, waiting for transfers between devices, local(): lax.psum_scatter(grad_qkv, ('dp', 'fsdp'), scatter_dimension=0, tiled=True)  104 us
  transfers between devices with their start and end apart: 16, of which 9 were waited for; matrix products, arithmetic and copies ran while one was open for 19% of the time, Pallas kernels for 0%

commit v1 on v0

--- a/solution.py
+++ b/solution.py
@@ -1,7 +1,372 @@
+import functools
+
 import jax
 import jax.numpy as jnp
 from jax import lax
+from jax.experimental import pallas as pl
+from jax.experimental.pallas import tpu as pltpu
 from jax.sharding import PartitionSpec as P
+
+MESH = pl.DeviceIdType.MESH
+CORES = 2
+
+
+def grid_sizes():
+    dp, fsdp = lax.axis_size("dp"), lax.axis_size("fsdp")
+    high = 2 if dp % 2 == 0 else 1
+    return (high, dp // high, fsdp // CORES, CORES)
+
+
+def own_place(sizes):
+    dp, fsdp = lax.axis_index("dp"), lax.axis_index("fsdp")
+    return (dp // sizes[1], dp % sizes[1], fsdp // CORES, fsdp % CORES)
+
+
+def peer_on(place, sizes, digit, step):
+    other = list(place)
+    other[digit] = (place[digit] + step) % sizes[digit]
+    return tuple(other)
+
+
+def device_of(place, sizes):
+    return (place[0] * sizes[1] + place[1], place[2] * CORES + place[3])
+
+
+def greet(place, sizes):
+    barrier = pltpu.get_barrier_semaphore()
+    met = 0
+    for digit in range(4):
+        for step in range(1, sizes[digit]):
+            other = peer_on(place, sizes, digit, step)
+            pl.semaphore_signal(
+                barrier, inc=1, device_id=device_of(other, sizes), device_id_type=MESH
+            )
+            met += 1
+    pl.semaphore_wait(barrier, met)
+
+
+def send(src, dst, sizes, other, send_sem, recv_sem):
+    copy = pltpu.make_async_remote_copy(
+        src_ref=src,
+        dst_ref=dst,
+        send_sem=send_sem,
+        recv_sem=recv_sem,
+        device_id=device_of(other, sizes),
+        device_id_type=MESH,
+    )
+    copy.start()
+    return copy
+
+
+def gather_kernel(sizes, *refs):
+    count = (len(refs) - 6) // 2
+    sources, gathered = refs[:count], refs[count : 2 * count]
+    local_sem, z_send, z_recv, hop_send, hop_recv, core_sem = refs[2 * count :]
+    place = own_place(sizes)
+    a, b, z, c = place
+    greet(place, sizes)
+    pending = []
+
+    def stage_z(i):
+        own = gathered[i].at[a, b, z, c]
+        keep = pltpu.make_async_copy(sources[i], own, local_sem.at[i])
+        keep.start()
+        copies = [
+            send(
+                sources[i],
+                own,
+                sizes,
+                peer_on(place, sizes, 2, step),
+                z_send.at[i, step - 1],
+                z_recv.at[i, step - 1],
+            )
+            for step in range(1, sizes[2])
+        ]
+        return keep, copies
+
+    def stage_hop(i, hop, digit, part):
+        return [
+            send(
+                part,
+                part,
+                sizes,
+                peer_on(place, sizes, digit, step),
+                hop_send.at[i, hop, step - 1],
+                hop_recv.at[i, hop, step - 1],
+            )
+            for step in range(1, sizes[digit])
+        ]
+
+    def finish(copies):
+        for copy in copies:
+            copy.wait_recv()
+        pending.extend(copies)
+
+    opened = [stage_z(i) for i in range(count)]
+    first, second, third = {}, {}, {}
+    for turn in range(count + 3):
+        if turn < count:
+            i = turn
+            opened[i][0].wait()
+            finish(opened[i][1])
+            first[i] = stage_hop(i, 0, 1 - i % 2, gathered[i].at[a, b, :, c])
+        i = turn - 1
+        if 0 <= i < count:
+            finish(first[i])
+            part = gathered[i].at[:, b, :, c] if i % 2 else gathered[i].at[a, :, :, c]
+            second[i] = stage_hop(i, 1, i % 2, part)
+        i = turn - 2
+        if 0 <= i < count:
+            finish(second[i])
+            part = gathered[i].at[:, :, :, c]
+            third[i] = [
+                send(
+                    part,
+                    part,
+                    sizes,
+                    peer_on(place, sizes, 3, 1),
+                    core_sem.at[i, 0],
+                    core_sem.at[i, 1],
+                )
+            ]
+        i = turn - 3
+        if 0 <= i < count:
+            finish(third[i])
+    for copy in pending:
+        copy.wait_send()
+
+
+def gather_all(shards):
+    sizes = grid_sizes()
+    count = len(shards)
+    steps = max(1, sizes[2] - 1)
+    wide = max(1, sizes[0] - 1, sizes[1] - 1)
+    dma = pltpu.SemaphoreType.DMA
+    return pl.pallas_call(
+        functools.partial(gather_kernel, sizes),
+        out_shape=[jax.ShapeDtypeStruct(sizes + s.shape, s.dtype) for s in shards],
+        in_specs=[pl.BlockSpec(memory_space=pl.ANY)] * count,
+        out_specs=[pl.BlockSpec(memory_space=pl.ANY)] * count,
+        scratch_shapes=[
+            dma((count,)),
+            dma((count, steps)),
+            dma((count, steps)),
+            dma((count, 2, wide)),
+            dma((count, 2, wide)),
+            dma((count, 2)),
+        ],
+        compiler_params=pltpu.CompilerParams(collective_id=0, has_side_effects=True),
+        name="gather_weights",
+    )(*shards)
+
+
+def scatter_kernel(sizes, *refs):
+    count = (len(refs) - 6) // 7
+    parts, owned = refs[:count], refs[count : 2 * count]
+    held, land_c, land_one, land_two, land_z = (
+        refs[(2 + j) * count : (3 + j) * count] for j in range(5)
+    )
+    core_sem, hop_send, hop_recv, z_send, z_recv, local_sem = refs[7 * count :]
+    place = own_place(sizes)
+    a, b, z, c = place
+    greet(place, sizes)
+    pending = []
+
+    def finish(copies):
+        for copy in copies:
+            copy.wait_recv()
+        pending.extend(copies)
+
+    def add_rows(total, pieces):
+        lead = total.shape[:-2]
+        steps = 1
+        for extent in lead:
+            steps *= extent
+
+        def body(at, carry):
+            index = []
+            rest = at
+            for extent in reversed(lead):
+                index.append(rest % extent)
+                rest = rest // extent
+            index = tuple(reversed(index))
+            value = total[index].astype(jnp.float32)
+            for piece in pieces:
+                value = value + piece[index].astype(jnp.float32)
+            total[index] = value.astype(total.dtype)
+            return carry
+
+        lax.fori_loop(0, steps, body, 0)
+
+    core_copies, keeps = [], []
+    for i in range(count):
+        core_copies.append(
+            [
+                send(
+                    parts[i].at[:, :, :, 1 - c],
+                    land_c[i],
+                    sizes,
+                    peer_on(place, sizes, 3, 1),
+                    core_sem.at[i, 0],
+                    core_sem.at[i, 1],
+                )
+            ]
+        )
+        keep = pltpu.make_async_copy(parts[i].at[:, :, :, c], held[i], local_sem.at[i])
+        keep.start()
+        keeps.append(keep)
+
+    def view(ref, digit, value):
+        return ref.at[value] if digit == 0 else ref.at[:, value]
+
+    def stage_hop(i, hop, digit, ref, axis, land):
+        copies = []
+        for step in range(1, sizes[digit]):
+            other = peer_on(place, sizes, digit, step)
+            copies.append(
+                send(
+                    view(ref, axis, other[digit]),
+                    land.at[step - 1],
+                    sizes,
+                    other,
+                    hop_send.at[i, hop, step - 1],
+                    hop_recv.at[i, hop, step - 1],
+                )
+            )
+        return copies
+
+    first, second, third = {}, {}, {}
+    for turn in range(count + 3):
+        if turn < count:
+            i = turn
+            keeps[i].wait()
+            finish(core_copies[i])
+            add_rows(held[i], [land_c[i]])
+            first[i] = stage_hop(i, 0, 1 - i % 2, held[i], 1 - i % 2, land_one[i])
+        i = turn - 1
+        if 0 <= i < count:
+            digit = 1 - i % 2
+            finish(first[i])
+            mine = view(held[i], digit, place[digit])
+            add_rows(mine, [land_one[i].at[s] for s in range(sizes[digit] - 1)])
+            second[i] = stage_hop(i, 1, 1 - digit, mine, 0, land_two[i])
+        i = turn - 2
+        if 0 <= i < count:
+            digit = 1 - i % 2
+            finish(second[i])
+            mine = view(held[i], digit, place[digit]).at[place[1 - digit]]
+            add_rows(mine, [land_two[i].at[s] for s in range(sizes[1 - digit] - 1)])
+            third[i] = []
+            for step in range(1, sizes[2]):
+                other = peer_on(place, sizes, 2, step)
+                third[i].append(
+                    send(
+                        mine.at[other[2]],
+                        land_z[i].at[step - 1],
+                        sizes,
+                        other,
+                        z_send.at[i, step - 1],
+                        z_recv.at[i, step - 1],
+                    )
+                )
+        i = turn - 3
+        if 0 <= i < count:
+            finish(third[i])
+            total = held[i][a, b, z].astype(jnp.float32)
+            for step in range(1, sizes[2]):
+                total = total + land_z[i][step - 1].astype(jnp.float32)
+            owned[i][...] = total
+    for copy in pending:
+        copy.wait_send()
+
+
+def scatter_all(parts):
+    sizes = grid_sizes()
+    count = len(parts)
+    steps = max(1, sizes[2] - 1)
+    wide = max(1, sizes[0] - 1, sizes[1] - 1)
+    dma = pltpu.SemaphoreType.DMA
+    blocks = [p.shape[4:] for p in parts]
+    lands = [[], [], [], [], []]
+    for i, block in enumerate(blocks):
+        digit = 1 - i % 2
+        other = sizes[1 - digit]
+        lands[0].append(pltpu.VMEM(sizes[:3] + block, jnp.bfloat16))
+        lands[1].append(pltpu.VMEM(sizes[:3] + block, jnp.bfloat16))
+        lands[2].append(
+            pltpu.VMEM((max(1, sizes[digit] - 1), other, sizes[2]) + block, jnp.bfloat16)
+        )
+        lands[3].append(pltpu.VMEM((max(1, other - 1), sizes[2]) + block, jnp.bfloat16))
+        lands[4].append(pltpu.VMEM((steps,) + block, jnp.bfloat16))
+    return pl.pallas_call(
+        functools.partial(scatter_kernel, sizes),
+        out_shape=[jax.ShapeDtypeStruct(block, jnp.float32) for block in blocks],
+        in_specs=[pl.BlockSpec(memory_space=pl.ANY)] * count,
+        out_specs=[pl.BlockSpec(memory_space=pltpu.VMEM)] * count,
+        scratch_shapes=lands[0]
+        + lands[1]
+        + lands[2]
+        + lands[3]
+        + lands[4]
+        + [
+            dma((count, 2)),
+            dma((count, 2, wide)),
+            dma((count, 2, wide)),
+            dma((count, steps)),
+            dma((count, steps)),
+            dma((count,)),
+        ],
+        compiler_params=pltpu.CompilerParams(
+            collective_id=1, has_side_effects=True, vmem_limit_bytes=56 * 2**20
+        ),
+        name="scatter_grads",
+    )(*parts)
+
+
+def total_kernel(sizes, value_ref, total_ref, *rest):
+    lands, (send_sem, recv_sem) = rest[:4], rest[4:]
+    place = own_place(sizes)
+    greet(place, sizes)
+    total_ref[...] = value_ref[...]
+    for stage, digit in enumerate((3, 2, 1, 0)):
+        if sizes[digit] == 1:
+            continue
+        copies = [
+            send(
+                total_ref,
+                lands[stage].at[step - 1],
+                sizes,
+                peer_on(place, sizes, digit, step),
+                send_sem.at[stage, step - 1],
+                recv_sem.at[stage, step - 1],
+            )
+            for step in range(1, sizes[digit])
+        ]
+        for copy in copies:
+            copy.wait()
+        total = total_ref[...]
+        for step in range(1, sizes[digit]):
+            total = total + lands[stage][step - 1]
+        total_ref[...] = total
+
+
+def total_of(values, ident):
+    sizes = grid_sizes()
+    dma = pltpu.SemaphoreType.DMA
+    return pl.pallas_call(
+        functools.partial(total_kernel, sizes),
+        out_shape=jax.ShapeDtypeStruct(values.shape, jnp.float32),
+        in_specs=[pl.BlockSpec(memory_space=pltpu.VMEM)],
+        out_specs=pl.BlockSpec(memory_space=pltpu.VMEM),
+        scratch_shapes=[
+            pltpu.VMEM((max(1, sizes[digit] - 1),) + values.shape, jnp.float32)
+            for digit in (3, 2, 1, 0)
+        ]
+        + [dma((4, max(sizes))), dma((4, max(sizes)))],
+        compiler_params=pltpu.CompilerParams(collective_id=ident, has_side_effects=True),
+        name=f"total_{ident}",
+    )(values)
+
 
 CTX = 128
 
@@ -252,36 +617,58 @@
     feature_mask = feature_keep(segments, time_spans[0], freq_spans[0], mel.shape[1])
     present = (segments >= 0).astype(jnp.float32)[:, None]
     counted = jnp.sum(lengths).astype(jnp.float32)
-    gathered = (
-        lax.all_gather(stem_kernels, ("dp", "fsdp"), axis=2, tiled=True),
-        lax.all_gather(stem_point, ("dp", "fsdp"), axis=1, tiled=True),
-        lax.all_gather(stem_out, ("dp", "fsdp"), axis=0, tiled=True),
-        lax.all_gather(ffn_in, ("dp", "fsdp"), axis=1, tiled=True),
-        lax.all_gather(ffn_out, ("dp", "fsdp"), axis=1, tiled=True),
-        lax.all_gather(qkv, ("dp", "fsdp"), axis=0, tiled=True),
-        lax.all_gather(attn_out, ("dp", "fsdp"), axis=0, tiled=True),
-        lax.all_gather(conv_in, ("dp", "fsdp"), axis=0, tiled=True),
-        lax.all_gather(conv_depth, ("dp", "fsdp"), axis=1, tiled=True),
-        lax.all_gather(conv_out, ("dp", "fsdp"), axis=0, tiled=True),
-        lax.all_gather(norm_gains, ("dp", "fsdp"), axis=1, tiled=True),
-        lax.all_gather(norm_shifts, ("dp", "fsdp"), axis=1, tiled=True),
-        lax.all_gather(final_shift, ("dp", "fsdp"), axis=0, tiled=True),
-    )
-    (
-        kernels,
-        point_weight,
-        stem_weight,
-        ffn_inner,
-        ffn_outer,
-        qkv_weight,
-        out_weight,
-        conv_inner,
-        conv_taps,
-        conv_outer,
-        norm_rows,
-        shift_rows,
-        final_row,
-    ) = gathered
+    small = jnp.concatenate(
+        [
+            part.astype(jnp.float32).reshape(-1)
+            for part in (stem_kernels, conv_depth, norm_gains, norm_shifts, final_shift)
+        ]
+    )
+    small = jnp.pad(small, (0, 1024 - small.shape[0])).reshape(8, 128)
+    bulk = gather_all(
+        [
+            small,
+            stem_point.astype(jnp.float32),
+            stem_out,
+            ffn_in[0],
+            ffn_out[0],
+            qkv,
+            attn_out,
+            conv_in,
+            conv_out,
+            ffn_in[1],
+            ffn_out[1],
+        ]
+    )
+    devices = lax.axis_size("dp") * lax.axis_size("fsdp")
+    flat = bulk[0].reshape(devices, 1024)
+    taken = 0
+
+    def spread(like):
+        nonlocal taken
+        size = like.size
+        piece = flat[:, taken : taken + size].reshape((devices,) + like.shape)
+        taken += size
+        piece = jnp.moveaxis(piece, 0, -2)
+        return piece.reshape(like.shape[:-1] + (devices * like.shape[-1],))
+
+    kernels = spread(stem_kernels)
+    conv_taps = spread(conv_depth)
+    norm_rows = spread(norm_gains)
+    shift_rows = spread(norm_shifts)
+    final_row = spread(final_shift)
+    point_weight = jnp.moveaxis(bulk[1].reshape((devices,) + stem_point.shape), 0, 1)
+    point_weight = point_weight.reshape(2, -1, stem_point.shape[2]).astype(jnp.bfloat16)
+
+    def rows_of(value):
+        return value.reshape(-1, value.shape[-1])
+
+    stem_weight = rows_of(bulk[2])
+    ffn_inner = (rows_of(bulk[3]), rows_of(bulk[9]))
+    ffn_outer = (rows_of(bulk[4]), rows_of(bulk[10]))
+    qkv_weight = rows_of(bulk[5])
+    out_weight = rows_of(bulk[6])
+    conv_inner = rows_of(bulk[7])
+    conv_outer = rows_of(bulk[8])
     kernels_wide = kernels.astype(jnp.float32)
     gains_wide = norm_rows.astype(jnp.float32)
     shifts_wide = shift_rows.astype(jnp.float32)
@@ -324,9 +711,11 @@
         gated_rows,
         taps_wide,
     )
-    first_sum, second_sum = lax.psum(
-        (jnp.sum(depthwise * present, axis=0), jnp.sum(depthwise * depthwise * present, axis=0)),
-        ("dp", "fsdp"),
+    first_sum, second_sum = total_of(
+        jnp.stack(
+            [jnp.sum(depthwise * present, axis=0), jnp.sum(depthwise * depthwise * present, axis=0)]
+        ),
+        2,
     )
     average = first_sum / counted
     spread = second_sum / counted - average * average
@@ -342,36 +731,9 @@
     activations = (layer_norm(after_second, gains_wide[5], final_wide) * present).astype(
         jnp.bfloat16
     )
-    weights_back = (
-        lax.all_gather(stem_kernels, ("dp", "fsdp"), axis=2, tiled=True),
-        lax.all_gather(stem_point, ("dp", "fsdp"), axis=1, tiled=True),
-        lax.all_gather(stem_out, ("dp", "fsdp"), axis=0, tiled=True),
-        lax.all_gather(ffn_in, ("dp", "fsdp"), axis=1, tiled=True),
-        lax.all_gather(ffn_out, ("dp", "fsdp"), axis=1, tiled=True),
-        lax.all_gather(qkv, ("dp", "fsdp"), axis=0, tiled=True),
-        lax.all_gather(attn_out, ("dp", "fsdp"), axis=0, tiled=True),
-        lax.all_gather(conv_in, ("dp", "fsdp"), axis=0, tiled=True),
-        lax.all_gather(conv_depth, ("dp", "fsdp"), axis=1, tiled=True),
-        lax.all_gather(conv_out, ("dp", "fsdp"), axis=0, tiled=True),
-        lax.all_gather(norm_gains, ("dp", "fsdp"), axis=1, tiled=True),
-        lax.all_gather(norm_shifts, ("dp", "fsdp"), axis=1, tiled=True),
-        lax.all_gather(final_shift, ("dp", "fsdp"), axis=0, tiled=True),
-    )
-    (
-        back_kernels,
-        back_point,
-        back_stem,
-        back_inner,
-        back_outer,
-        back_qkv,
-        back_attn,
-        back_conv_in,
-        back_taps,
-        back_conv_out,
-        back_gains,
-        back_shifts,
-        back_final,
-    ) = weights_back
+    back_point, back_stem, back_inner, back_outer = point_weight, stem_weight, ffn_inner, ffn_outer
+    back_qkv, back_attn, back_conv_in, back_conv_out = qkv_weight, out_weight, conv_inner, conv_outer
+    back_gains, back_shifts, back_final = norm_rows, shift_rows, final_row
     back_gains_wide = back_gains.astype(jnp.float32)
     back_shifts_wide = back_shifts.astype(jnp.float32)
     back_final_wide = back_final.astype(jnp.float32)
@@ -392,9 +754,14 @@
     grad_conv_out = over_rows(conv_active, grad_conv_low)
     grad_active = against(grad_conv_low, back_conv_out)
     grad_batch = jax.vjp(jax.nn.silu, batch_normed)[1](grad_active)[0]
-    beta_sum, gamma_sum = lax.psum(
-        (jnp.sum(grad_batch * present, axis=0), jnp.sum(grad_batch * standard * present, axis=0)),
-        ("dp", "fsdp"),
+    beta_sum, gamma_sum = total_of(
+        jnp.stack(
+            [
+                jnp.sum(grad_batch * present, axis=0),
+                jnp.sum(grad_batch * standard * present, axis=0),
+            ]
+        ),
+        3,
     )
     bn_gain = back_gains_wide[3]
     grad_first = (
@@ -451,44 +818,72 @@
     )
     grad_kernels = jnp.stack([grad_first_kernel, grad_second_kernel, grad_third_kernel])
     grad_points = jnp.stack([grad_second_point, grad_third_point])
-    grad_inner = jnp.stack([ffn_one[3], ffn_two[3]])
-    grad_outer = jnp.stack([ffn_one[4], ffn_two[4]])
-    owned_grads = (
-        lax.psum_scatter(grad_kernels, ("dp", "fsdp"), scatter_dimension=2, tiled=True),
-        lax.psum_scatter(grad_points, ("dp", "fsdp"), scatter_dimension=1, tiled=True),
-        lax.psum_scatter(grad_stem_out, ("dp", "fsdp"), scatter_dimension=0, tiled=True),
-        lax.psum_scatter(grad_inner, ("dp", "fsdp"), scatter_dimension=1, tiled=True),
-        lax.psum_scatter(grad_outer, ("dp", "fsdp"), scatter_dimension=1, tiled=True),
-        lax.psum_scatter(grad_qkv, ("dp", "fsdp"), scatter_dimension=0, tiled=True),
-        lax.psum_scatter(grad_attn_out, ("dp", "fsdp"), scatter_dimension=0, tiled=True),
-        lax.psum_scatter(grad_conv_in, ("dp", "fsdp"), scatter_dimension=0, tiled=True),
-        lax.psum_scatter(grad_taps, ("dp", "fsdp"), scatter_dimension=1, tiled=True),
-        lax.psum_scatter(grad_conv_out, ("dp", "fsdp"), scatter_dimension=0, tiled=True),
-        lax.psum_scatter(grad_gains, ("dp", "fsdp"), scatter_dimension=1, tiled=True),
-        lax.psum_scatter(grad_shifts, ("dp", "fsdp"), scatter_dimension=1, tiled=True),
-        lax.psum_scatter(grad_shift_final, ("dp", "fsdp"), scatter_dimension=0, tiled=True),
-    )
-    share_width = gamma_sum.shape[0] // (lax.axis_size("dp") * lax.axis_size("fsdp"))
+    sizes = grid_sizes()
+
+    def blocks_of(value):
+        rows = value.shape[0] // devices
+        return value.astype(jnp.bfloat16).reshape(sizes + (rows, value.shape[1]))
+
+    points_low = grad_points.astype(jnp.bfloat16).reshape(2, devices, -1, channels)
+    points_low = jnp.moveaxis(points_low, 0, 1).reshape(sizes + (-1, channels))
+    owned = scatter_all(
+        [
+            blocks_of(ffn_two[3]),
+            blocks_of(ffn_two[4]),
+            blocks_of(grad_conv_out),
+            blocks_of(grad_conv_in),
+            blocks_of(grad_attn_out),
+            blocks_of(grad_qkv),
+            blocks_of(ffn_one[3]),
+            blocks_of(ffn_one[4]),
+            blocks_of(grad_stem_out),
+            points_low,
+        ]
+    )
+    pieces = [
+        grad_kernels.reshape(-1),
+        grad_taps.reshape(-1),
+        grad_gains.reshape(-1),
+        grad_shifts.reshape(-1),
+        grad_shift_final.reshape(-1),
+    ]
+    joined_small = jnp.concatenate(pieces)
+    extra = -joined_small.shape[0] % 4096
+    summed_small = total_of(jnp.pad(joined_small, (0, extra)).reshape(-1, 512), 4).reshape(-1)
+    taken = 0
+
+    def own_share(like):
+        nonlocal taken
+        size = like.size
+        piece = summed_small[taken : taken + size].reshape(like.shape)
+        taken += size
+        width = like.shape[-1] // devices
+        return lax.dynamic_slice_in_dim(piece, device * width, width, axis=like.ndim - 1)
+
+    own_kernels = own_share(grad_kernels)
+    own_taps = own_share(grad_taps)
+    own_gains = own_share(grad_gains)
+    own_shifts = own_share(grad_shifts)
+    own_final = own_share(grad_shift_final)
+    share_width = gamma_sum.shape[0] // devices
     own_gamma = lax.dynamic_slice_in_dim(gamma_sum, device * share_width, share_width)
     own_beta = lax.dynamic_slice_in_dim(beta_sum, device * share_width, share_width)
-    owned_gains = owned_grads[10].at[3].add(own_gamma)
-    owned_shifts = owned_grads[11].at[3].add(own_beta)
     return (
         activations,
         mel_grad,
-        owned_grads[0],
-        owned_grads[1],
-        owned_grads[2],
-        owned_grads[3],
-        owned_grads[4],
-        owned_grads[5],
-        owned_grads[6],
-        owned_grads[7],
-        owned_grads[8],
-        owned_grads[9],
-        owned_gains,
-        owned_shifts,
-        owned_grads[12],
+        own_kernels,
+        owned[9].reshape(stem_point.shape),
+        owned[8],
+        jnp.stack([owned[6], owned[0]]),
+        jnp.stack([owned[7], owned[1]]),
+        owned[5],
+        owned[4],
+        owned[3],
+        own_taps,
+        owned[2],
+        own_gains.at[3].add(own_gamma),
+        own_shifts.at[3].add(own_beta),
+        own_final,
     )
 
 

time: 2170 us -> 734 us (0.34)
  waiting for transfers between devices: 1190 us -> 0 us
  blocking collectives: 449 us -> 0 us
  Pallas kernels: 0 us -> 242 us
    reduce_scatter x8 -> x0, waiting for transfers between devices: 1090 us -> none  [the longest x1 153 us: local(): lax.psum_scatter(grad_inner, ('dp', 'fsdp'), scatter_dimension=1, tiled=T...]
    all_gather x7 -> x0, blocking collectives: 283 us -> none  [the longest x1 44.3 us: local(): lax.all_gather(stem_kernels, ('dp', 'fsdp'), axis=2, tiled=True)]
    pallas_call x0 -> x5, Pallas kernels: none -> 242 us  [the longest x1 97.3 us: gather_all(): pl.pallas_call(functools.partial(gather_kernel, sizes), out_shape=[jax.Sh...]
    unnamed x19 -> x0, waiting for transfers between devices: 102 us -> none
    unnamed x2 -> x0, blocking collectives: 86.1 us -> none
    psum x2 -> x0, blocking collectives: 79.8 us -> none  [the longest x1 41.6 us: local(): lax.psum((jnp.sum(grad_batch * present, axis=0), jnp.sum(grad_batch * sta...]
  transfers between devices with their start and end apart: 16 -> 0, of which waited for: 9 -> 0; matrix products, arithmetic and copies ran while one was open for 19% -> 0% of each run, Pallas kernels for 0% -> 0%
where the time goes in v1:
time: 734 us; the launch traced here: 726 us
  Pallas kernels  242 us (33%)
  other arithmetic  236 us (32%)
  local copies, waits for them, and re-layouts  164 us (22%)
  matrix products  78.7 us (11%)
    reduce_sum x3, other arithmetic, strided_conv(): addend = tap_piece * kernel[3 * tap_row + tap_col]  99.9 us
    pallas_call x1, Pallas kernels, gather_all(): pl.pallas_call(functools.partial(gather_kernel, sizes), out_shape=[jax.Sh...  97.3 us
    pallas_call x1, Pallas kernels, scatter_all(): pl.pallas_call(functools.partial(scatter_kernel, sizes), out_shape=[jax.S...  95.8 us
    pallas_call x3, Pallas kernels, total_of(): pl.pallas_call(functools.partial(total_kernel, sizes), out_shape=jax.Shap...  48.9 us
    unnamed x483, local copies, waits for them, and re-layouts  28.7 us
    mul x1, other arithmetic, stem_front(): jax.nn.silu(strided_conv(masked, first_kernel, seg_zero, seg_one))  27.7 us
    dot_general x11, matrix products, over_rows(): lax.dot_general(operand, matrix, (((0,), (0,)), ((), ())), preferred_elem...  22.5 us
    convert_element_type x1, other arithmetic, local(): level_two_low = level_two.reshape(-1, channels).astype(jnp.bfloat16)  18.8 us

profile of v1, /device:TPU:0, one launch (start us, length us, event | category | flops | bytes accessed | tf_op | source)
XLA Modules:
  0.0 725.9 jit_solution(13540846262094817650)
XLA Ops:
  25.3 97.3 %gather_weights.1 = (f32[2,2,4,2,8,128]{5,4,3,2,1,0:T(8,128)}, f32[2,2,4,2,2,8,256]{6,5,4,3,2,1,0:T(8,128)}, bf16[2,2,4,2,80,512]{5,4,3,2,1,0:T(8,128)(2,1)}, bf...) custom-call(f32[8,128]{1,0:T(8,128)} %bitcast_convert_fusion.refs_0_, ...), custom_call_target="tpu_custom_call" | custom-call | tf_op jit(solution)/shard_map/gather_weights/pallas_call | solution.py:145
  148.6 27.7 %fusion.4 = f32[256,2,40,256]{3,0,2,1:T(8,128)} fusion(f32[256]{0:T(256)S(1)} %get-tuple-element.389, f32[256]{0:T(256)S(1)} %mul.1946, f32[256,2,40]{0,2,1:T(8,128)S(1)} %copy.566, f32[256]{0:T(256)S(1)} %mul.1941, f32[256,2,40]{0,2,1:T(8,128)S(1)} %copy.563, f32[256]{0:T(256)S(1)} %mul.1936, f32[256,2,40]{0,2,1:T(8,128)S(1)} %copy.560, f32[256]{0:T(256)S(1)} %mul.1931, ...), kind=kLoop, calls=%fused_computation.24 | loop fusion | flops 115343360 | bytes 21719040 | tf_op jit(solution)/shard_map/jvp(jit(silu))/mul | solution.py:468
  181.2 5.4 pad_multiply_fusion
  186.6 8.4 %fusion.137 = (f32[256,1,40,256]{3,0,2,1:T(8,128)S(1)}, f32[256,1,40,256]{3,0,2,1:T(8,128)S(1)}) fusion(f32[256,2,40,256]{3,0,2,1:T(8,128)} %fusion.4), kind=kLoop, calls=%fused_computation.428 | loop fusion | bytes 41943040 | tf_op jit(solution)/shard_map/jvp()/slice | solution.py:407
  212.3 18.8 %multiply_convert_fusion = bf16[256,20,256]{2,0,1:T(8,128)(2,1)} fusion(f32[256,19,256]{2,0,1:T(8,128)} %slice.738, f32[256,19,256]{2,0,1:T(8,128)} %slice.731, f32[256,19,256]{2,0,1:T(8,128)} %slice.724, f32[256,20,2,256]{3,0,2,1:T(8,128)} %bitcast.484, f32[256,20,2,256]{3,0,2,1:T(8,128)} %bitcast.479, f32[256,20,2,256]{3,0,2,1:T(8,128)} %bitcast.482, ...), kind=kLoop, calls=%fused_computation.61 | loop fusion | flops 24903680 | bytes 49031168 | tf_op jit(solution)/shard_map/convert_element_type | solution.py:686
  241.4 5.4 fusion.8
  246.8 6.7 reshape.1572
  288.8 15.5 %total_2.1 = f32[2,512]{1,0:T(2,128)} custom-call(f32[2,512]{1,0:T(2,128)} %pad_maximum_fusion.3.value_ref), custom_call_target="tpu_custom_call" | custom-call | tf_op jit(solution)/shard_map/total_2/pallas_call | solution.py:356
  315.0 13.6 %total_3.1 = f32[2,512]{1,0:T(2,128)} custom-call(f32[2,512]{1,0:T(2,128)} %pad_maximum_fusion.4.value_ref), custom_call_target="tpu_custom_call" | custom-call | tf_op jit(solution)/shard_map/total_3/pallas_call | solution.py:356
  355.5 9.1 %fusion.34 = bf16[128,1,8,64]{0,3,2,1:T(8,128)(2,1)} fusion(f32[8,128,384]{2,1,0:T(8,128)} %fusion.68, f32[8,128,384]{2,1,0:T(8,128)} %copy-done.22, f32[8,128]{1,0:T(8,128)S(1)} %copy-done.111, bf16[128,8,64]{0,2,1:T(8,128)(2,1)S(1)} %copy-done.81), kind=kOutput, calls=%fused_computation.137 | convolution fusion | flops 53085568 | bytes 3411968 | tf_op jit(solution)/shard_map/hqk,khd->qhd/dot_general | solution.py:572
  364.6 9.3 %fusion.29 = bf16[384,8,64]{0,2,1:T(8,128)(2,1)} fusion(f32[8,128,384]{2,1,0:T(8,128)} %fusion.68, f32[8,128,384]{2,1,0:T(8,128)} %copy-done.22, f32[8,128]{1,0:T(8,128)S(1)} %copy-done.111, bf16[128,3,8,64]{0,3,2,1:T(8,128)(2,1)} %bitcast.540), kind=kOutput, calls=%fused_computation.128 | convolution fusion | flops 53085568 | bytes 6823936 | tf_op jit(solution)/shard_map/hqk,qhd->khd/dot_general | solution.py:576
  412.5 5.8 copy.633
  418.3 6.8 reshape.1592
  425.1 5.4 fusion.7
  432.1 95.8 %scatter_grads.1 = (f32[16,2048]{1,0:T(8,128)}, f32[64,512]{1,0:T(8,128)}, f32[16,512]{1,0:T(8,128)}, f32[16,1024]{1,0:T(8,128)}, f32[16,512]{1,0:T(8,128)}, /*i...) custom-call(bf16[2,2,4,2,16,2048]{5,4,3,2,1,0:T(8,128)(2,1)} %bitcast.51, ...), custom_call_target="tpu_custom_call" | custom-call | tf_op jit(solution)/shard_map/scatter_grads/pallas_call | solution.py:301
  536.7 5.9 slice_multiply_fusion.2
  542.6 32.7 %multiply_reduce_fusion.26 = (f32[256]{0:T(256)S(1)}, f32[256]{0:T(256)S(1)}, f32[256]{0:T(256)S(1)}, f32[256]{0:T(256)S(1)}, f32[256]{0:T(256)S(1)}, /*index=5*...) fusion(f32[256,20,256]{2,0,1:T(8,128)S(1)} %broadcast_multiply_, ...), kind=kLoop, calls=%fused_computation.51 | loop fusion | flops 35387136 | bytes 98057216 | tf_op jit(solution)/shard_map/transpose(jvp())/reduce_sum | solution.py:432
  575.4 4.9 pad_add_fusion
  585.1 4.9 pad_add_fusion.1
  594.7 9.4 %slice_multiply_fusion = f32[255,40,256]{2,0,1:T(8,128)} fusion(f32[256,40,256]{2,0,1:T(8,128)} %bitcast.491, f32[255]{0:T(256)S(1)} %copy-done.203), kind=kLoop, calls=%fused_computation.26 | loop fusion | flops 2611200 | bytes 20890620 | tf_op jit(solution)/shard_map/transpose(jvp())/mul | solution.py:414
  604.1 4.9 pad_add_fusion.2
  613.9 12.9 %bitcast_add_fusion = f32[256,40,256]{2,0,1:T(8,128)} fusion(f32[256,20,2,256]{3,0,2,1:T(8,128)} %copy.635, f32[255,40,256]{2,0,1:T(8,128)} %slice_multiply_fusion), kind=kLoop, calls=%fused_computation.28 | loop fusion | flops 2621440 | bytes 31416320 | tf_op jit(solution)/shard_map/transpose(jvp())/add_any | solution.py:409
  627.0 64.5 %multiply_reduce_fusion.8 = (f32[256]{0:T(256)S(1)}, f32[256]{0:T(256)S(1)}, f32[256]{0:T(256)S(1)}, f32[256]{0:T(256)S(1)}, f32[256]{0:T(256)S(1)}, /*index=5*/...) fusion(f32[256,2,40]{0,2,1:T(8,128)S(1)} %copy-done.57, ...), kind=kLoop, calls=%fused_computation.13 | loop fusion | flops 340600576 | bytes 22465536 | tf_op jit(solution)/shard_map/transpose(jvp())/reduce_sum | solution.py:432
  692.3 19.8 %total_4.1 = f32[40,512]{1,0:T(8,128)} custom-call(f32[40,512]{1,0:T(8,128)} %reshape.1625.value_ref), custom_call_target="tpu_custom_call" | custom-call | tf_op jit(solution)/shard_map/total_4/pallas_call | solution.py:356
  (863 shorter events, 229.0 us)
Async XLA Ops:
  14.0 198.3 %copy-start.89 = (f32[256]{0:T(256)}, f32[256]{0:T(256)S(1)}, u32[]{:S(2)}) copy-start(f32[256]{0:T(256)S(1)} %get-tuple-element.389) | copy-start | bytes 3076
  22.9 125.6 %copy-start.54 = (f32[256,2,40]{0,2,1:T(8,128)}, f32[256,2,40]{0,2,1:T(8,128)S(1)}, u32[]{:S(2)}) copy-start(f32[256,2,40]{0,2,1:T(8,128)S(1)} %copy.560) | copy-start | bytes 245764
  23.2 125.3 %copy-start.56 = (f32[256,2,40]{0,2,1:T(8,128)}, f32[256,2,40]{0,2,1:T(8,128)S(1)}, u32[]{:S(2)}) copy-start(f32[256,2,40]{0,2,1:T(8,128)S(1)} %copy.566) | copy-start | bytes 245764
  23.5 125.1 %copy-start.58 = (f32[256,2,40]{0,2,1:T(8,128)}, f32[256,2,40]{0,2,1:T(8,128)S(1)}, u32[]{:S(2)}) copy-start(f32[256,2,40]{0,2,1:T(8,128)S(1)} %copy.563) | copy-start | bytes 245764
  23.9 124.7 %copy-start.60 = (f32[256,2,40]{0,2,1:T(8,128)}, f32[256,2,40]{0,2,1:T(8,128)S(1)}, u32[]{:S(2)}) copy-start(f32[256,2,40]{0,2,1:T(8,128)S(1)} %copy.550) | copy-start | bytes 245764
  24.1 124.4 %copy-start.62 = (f32[256,2,40]{0,2,1:T(8,128)}, f32[256,2,40]{0,2,1:T(8,128)S(1)}, u32[]{:S(2)}) copy-start(f32[256,2,40]{0,2,1:T(8,128)S(1)} %copy.556) | copy-start | bytes 245764
  24.4 124.1 %copy-start.64 = (f32[256,2,40]{0,2,1:T(8,128)}, f32[256,2,40]{0,2,1:T(8,128)S(1)}, u32[]{:S(2)}) copy-start(f32[256,2,40]{0,2,1:T(8,128)S(1)} %copy.553) | copy-start | bytes 245764
  24.7 123.9 %copy-start.66 = (f32[256,2,40]{0,2,1:T(8,128)}, f32[256,2,40]{0,2,1:T(8,128)S(1)}, u32[]{:S(2)}) copy-start(f32[256,2,40]{0,2,1:T(8,128)S(1)} %copy.544) | copy-start | bytes 245764
  25.0 151.2 %copy-start.68 = (f32[256,2,40]{0,2,1:T(8,128)}, f32[256,2,40]{0,2,1:T(8,128)S(1)}, u32[]{:S(2)}) copy-start(f32[256,2,40]{0,2,1:T(8,128)S(1)} %copy.546) | copy-start | bytes 245764
  25.2 151.0 %copy-start.70 = (f32[256,2,40]{0,2,1:T(8,128)}, f32[256,2,40]{0,2,1:T(8,128)S(1)}, u32[]{:S(2)}) copy-start(f32[256,2,40]{0,2,1:T(8,128)S(1)} %copy.539) | copy-start | bytes 245764
  146.2 66.1 %copy-start.139 = (f32[256]{0:T(256)}, f32[256]{0:T(256)S(1)}, u32[]{:S(2)}) copy-start(f32[256]{0:T(256)S(1)} %mul.1978) | copy-start | bytes 3076
  146.3 65.9 %copy-start.141 = (f32[256]{0:T(256)}, f32[256]{0:T(256)S(1)}, u32[]{:S(2)}) copy-start(f32[256]{0:T(256)S(1)} %mul.1975) | copy-start | bytes 3076
  146.5 65.7 %copy-start.169 = (f32[256]{0:T(256)}, f32[256]{0:T(256)S(1)}, u32[]{:S(2)}) copy-start(f32[256]{0:T(256)S(1)} %mul.1972) | copy-start | bytes 3076
  146.7 65.6 %copy-start.143 = (f32[256]{0:T(256)}, f32[256]{0:T(256)S(1)}, u32[]{:S(2)}) copy-start(f32[256]{0:T(256)S(1)} %mul.1969) | copy-start | bytes 3076
  146.9 65.4 %copy-start.145 = (f32[256]{0:T(256)}, f32[256]{0:T(256)S(1)}, u32[]{:S(2)}) copy-start(f32[256]{0:T(256)S(1)} %mul.1966) | copy-start | bytes 3076
  147.0 65.2 %copy-start.171 = (f32[256]{0:T(256)}, f32[256]{0:T(256)S(1)}, u32[]{:S(2)}) copy-start(f32[256]{0:T(256)S(1)} %mul.1963) | copy-start | bytes 3076
  147.2 65.1 %copy-start.147 = (f32[256]{0:T(256)}, f32[256]{0:T(256)S(1)}, u32[]{:S(2)}) copy-start(f32[256]{0:T(256)S(1)} %mul.1960) | copy-start | bytes 3076
  147.4 64.9 %copy-start.149 = (f32[256]{0:T(256)}, f32[256]{0:T(256)S(1)}, u32[]{:S(2)}) copy-start(f32[256]{0:T(256)S(1)} %mul.1957) | copy-start | bytes 3076
  147.6 64.7 %copy-start.173 = (f32[256]{0:T(256)}, f32[256]{0:T(256)S(1)}, u32[]{:S(2)}) copy-start(f32[256]{0:T(256)S(1)} %mul.1954) | copy-start | bytes 3076
  284.5 60.0 %copy-start.113 = (f32[128]{0:T(128)}, f32[128]{0:T(128)S(1)}, u32[]{:S(2)}) copy-start(f32[128]{0:T(128)S(1)} %broadcast_multiply_fusion.4) | copy-start | bytes 1540
  284.7 59.8 %copy-start.175 = (f32[128]{0:T(128)}, f32[128]{0:T(128)S(1)}, u32[]{:S(2)}) copy-start(f32[128]{0:T(128)S(1)} %fusion.113) | copy-start | bytes 1540
  626.9 64.6 %copy-start.84 = (f32[17664]{0:T(1024)S(1)}, f32[17664]{0:T(1024)}, u32[]{:S(2)}) copy-start(f32[17664]{0:T(1024)} %custom-call) | copy-start | bytes 211972
  626.9 64.6 %copy-start.83 = (f32[4608]{0:T(1024)S(1)}, f32[4608]{0:T(1024)}, u32[]{:S(2)}) copy-start(f32[4608]{0:T(1024)} %reshape.1613) | copy-start | bytes 55300
  626.9 64.7 %copy-start.188 = (f32[512]{0:T(512)S(1)}, f32[512]{0:T(512)}, u32[]{:S(2)}) copy-start(f32[512]{0:T(512)} %get-tuple-element.267) | copy-start | bytes 6148
  (204 other events, 1319.9 us)
